TPU v7x, 32 devices: a whole 2x2x4 slice. The times are simulated.
32 devices in a mesh: dp: 8 (over y, x, core), seq: 4 (over z).
Axes of the slice: x: 2, y: 2, z: 4, core: 2. Of those that a mesh axis runs over, the one named last changes fastest.
Arguments:
- tokens: bfloat16 [8, 1024, 1280], P('dp', 'seq'), may hold values from -6 to 6
- cotangent: bfloat16 [8, 1024, 1280], P('dp', 'seq'), may hold values from -6 to 6
- weight_inproj: float32 [1, 1280, 3840], P(None, 'dp', 'seq'), may hold values from -0.15625 to 0.15625
- first_inproj: float32 [1, 1280, 3840], P(None, 'dp', 'seq'), may hold values from -8 to 8
- second_inproj: float32 [1, 1280, 3840], P(None, 'dp', 'seq'), may hold values from 9.68 to 38.48
- weight_outproj: float32 [1, 1280, 1280], P(None, 'dp', 'seq'), may hold values from -0.625 to 0.625
- first_outproj: float32 [1, 1280, 1280], P(None, 'dp', 'seq'), may hold values from -16 to 16
- second_outproj: float32 [1, 1280, 1280], P(None, 'dp', 'seq'), may hold values from 38.5024 to 155.648
- weight_expand: float32 [1, 1280, 5120], P(None, 'dp', 'seq'), may hold values from -0.15625 to 0.15625
- first_expand: float32 [1, 1280, 5120], P(None, 'dp', 'seq'), may hold values from -16 to 16
- second_expand: float32 [1, 1280, 5120], P(None, 'dp', 'seq'), may hold values from 38.5024 to 155.648
- weight_contract: float32 [1, 5120, 1280], P(None, 'dp', 'seq'), may hold values from -0.078125 to 0.078125
- first_contract: float32 [1, 5120, 1280], P(None, 'dp', 'seq'), may hold values from -32 to 32
- second_contract: float32 [1, 5120, 1280], P(None, 'dp', 'seq'), may hold values from 155.648 to 622.592
- gain_values: float32 [1, 2, 1280], replicated, may hold values from 0.1 to 1.9
- first_gains: float32 [1, 2, 1280], replicated, may hold values from -40 to 40
- second_gains: float32 [1, 2, 1280], replicated, may hold values from 211.3536 to 843.776
- bias_values: float32 [1, 10, 1280], replicated, may hold values from -4 to 4
- first_biases: float32 [1, 10, 1280], replicated, may hold values from -32 to 32
- second_biases: float32 [1, 10, 1280], replicated, may hold values from 108.1344 to 430.8992
Outputs:
- block_out: float32 [8, 1024, 1280], P('dp', 'seq')
- grad_tokens: float32 [8, 1024, 1280], P('dp', 'seq')
- gradient_inproj: float32 [1, 1280, 3840], P(None, 'dp', 'seq')
- momentum_inproj: float32 [1, 1280, 3840], P(None, 'dp', 'seq')
- variance_inproj: float32 [1, 1280, 3840], P(None, 'dp', 'seq')
- updated_inproj: float32 [1, 1280, 3840], P(None, 'dp', 'seq')
- gradient_outproj: float32 [1, 1280, 1280], P(None, 'dp', 'seq')
- momentum_outproj: float32 [1, 1280, 1280], P(None, 'dp', 'seq')
- variance_outproj: float32 [1, 1280, 1280], P(None, 'dp', 'seq')
- updated_outproj: float32 [1, 1280, 1280], P(None, 'dp', 'seq')
- gradient_expand: float32 [1, 1280, 5120], P(None, 'dp', 'seq')
- momentum_expand: float32 [1, 1280, 5120], P(None, 'dp', 'seq')
- variance_expand: float32 [1, 1280, 5120], P(None, 'dp', 'seq')
- updated_expand: float32 [1, 1280, 5120], P(None, 'dp', 'seq')
- gradient_contract: float32 [1, 5120, 1280], P(None, 'dp', 'seq')
- momentum_contract: float32 [1, 5120, 1280], P(None, 'dp', 'seq')
- variance_contract: float32 [1, 5120, 1280], P(None, 'dp', 'seq')
- updated_contract: float32 [1, 5120, 1280], P(None, 'dp', 'seq')
- gradient_gains: float32 [1, 2, 1280], replicated
- momentum_gains: float32 [1, 2, 1280], replicated
- variance_gains: float32 [1, 2, 1280], replicated
- updated_gains: float32 [1, 2, 1280], replicated
- gradient_biases: float32 [1, 10, 1280], replicated
- momentum_biases: float32 [1, 10, 1280], replicated
- variance_biases: float32 [1, 10, 1280], replicated
- updated_biases: float32 [1, 10, 1280], replicated
All inputs are finite; a program needn't handle non-finite values.
Results may differ from a plain program's by a relative error of at most 0.01.
Values may be sent and summed in bfloat16 or wider, within the bound.
No kernel may reach another device: no remote copies, remote signals or barrier semaphores. Data moves between devices by JAX's collectives and lax.ppermute only.
A program may use at most 320 MiB of HBM per device.

v0:
```python
import jax
import jax.numpy as jnp
from jax import lax
from jax.sharding import PartitionSpec as P

HEADS = 20
HEAD_DIM = 64
STEP = 10


NORM_EPS = 1e-05
BETA_ONE = 0.9
BETA_TWO = 0.95
ADAM_EPS = 1e-08
MATRIX_RATE = 0.02
VECTOR_RATE = 0.15
MATRIX_DECAY = 0.1
CONTRACT_LAST = (((1,), (1,)), ((), ()))
CONTRACT_FIRST = (((0,), (0,)), ((), ()))


def layer_norm(values, gain, shift):
    center = values - jnp.mean(values, axis=-1, keepdims=True)
    spread = jnp.mean(center * center, axis=-1, keepdims=True)
    return center * lax.rsqrt(spread + NORM_EPS) * gain + shift


def smooth_gate(values):
    return jax.nn.gelu(values, approximate=True)


def fetch_layer(inproj, outproj, expand, contract):
    inproj = inproj.astype(jnp.bfloat16)
    outproj = outproj.astype(jnp.bfloat16)
    expand = expand.astype(jnp.bfloat16)
    contract = contract.astype(jnp.bfloat16)
    lengthened = (
        lax.all_gather(inproj, "dp", axis=0, tiled=True),
        lax.all_gather(outproj, "dp", axis=0, tiled=True),
        lax.all_gather(expand, "dp", axis=0, tiled=True),
        lax.all_gather(contract, "dp", axis=0, tiled=True),
    )
    result = (
        lax.all_gather(lengthened[0], "seq", axis=1, tiled=True),
        lax.all_gather(lengthened[1], "seq", axis=1, tiled=True),
        lax.all_gather(lengthened[2], "seq", axis=1, tiled=True),
        lax.all_gather(lengthened[3], "seq", axis=1, tiled=True),
    )
    return result


def reduce_weight(left, right):
    summed_rows = lax.psum_scatter(
        lax.dot_general(left, right, CONTRACT_FIRST, preferred_element_type=jnp.float32),
        "dp",
        scatter_dimension=0,
        tiled=True,
    )
    return lax.psum_scatter(summed_rows, "seq", scatter_dimension=1, tiled=True)


def split_heads(both, width):
    keyed = both[:, :width].reshape(both.shape[0], HEADS, HEAD_DIM)
    valued = both[:, width:].reshape(both.shape[0], HEADS, HEAD_DIM)
    return (keyed, valued)


def masked_scores(query, keyed, offset):
    scores = jnp.einsum(
        "qhd,khd->hqk", query, keyed, preferred_element_type=jnp.float32
    ) * HEAD_DIM ** (-0.5)
    rowpos = offset + lax.broadcasted_iota(jnp.int32, scores.shape, 1)
    colpos = lax.broadcasted_iota(jnp.int32, scores.shape, 2)
    return jnp.where(colpos <= rowpos, scores, -1000000000.0)


def attend_forward(query, both, offset):
    width = HEADS * HEAD_DIM
    keyed, valued = split_heads(both, width)
    scores = masked_scores(query, keyed, offset)
    topmost = jnp.max(scores, axis=-1, keepdims=True)
    totals = jnp.sum(jnp.exp(scores - topmost), axis=-1, keepdims=True)
    logsum = topmost + jnp.log(totals)
    probs = jnp.exp(scores - logsum).astype(jnp.bfloat16)
    output = jnp.einsum("hqk,khd->qhd", probs, valued, preferred_element_type=jnp.float32)
    return (output.reshape(query.shape[0], width).astype(jnp.bfloat16), logsum)


def attend_backward(query, both, logsum, grad_incoming, offset):
    width = HEADS * HEAD_DIM
    keyed, valued = split_heads(both, width)
    scores = masked_scores(query, keyed, offset)
    probs = jnp.exp(scores - logsum)
    grad_heads = grad_incoming.reshape(query.shape)
    grad_probs = jnp.einsum("qhd,khd->hqk", grad_heads, valued, preferred_element_type=jnp.float32)
    grad_scores = probs * (grad_probs - jnp.sum(grad_probs * probs, axis=-1, keepdims=True))
    grad_scores = grad_scores.astype(jnp.bfloat16)
    scale_factor = HEAD_DIM ** (-0.5)
    grad_query = (
        jnp.einsum("hqk,khd->qhd", grad_scores, keyed, preferred_element_type=jnp.float32)
        * scale_factor
    )
    grad_key = (
        jnp.einsum("hqk,qhd->khd", grad_scores, query, preferred_element_type=jnp.float32)
        * scale_factor
    )
    grad_value = jnp.einsum(
        "hqk,qhd->khd", probs.astype(jnp.bfloat16), grad_heads, preferred_element_type=jnp.float32
    )
    length = both.shape[0]
    grad_pairs = jnp.concatenate(
        [grad_key.reshape(length, width), grad_value.reshape(length, width)], axis=1
    )
    return (grad_query.reshape(query.shape[0], width), grad_pairs)


def forward_layer(inputs, weights, gains, shifts, offset):
    inproj, outproj, expand, contract = weights
    seqs, local, width = inputs.shape
    rows_in = inputs.reshape(seqs * local, width)
    normed = layer_norm(rows_in, gains[0], shifts[0]).astype(jnp.bfloat16)
    blank = jnp.zeros_like(shifts[1])
    joined = jnp.dot(normed, inproj, preferred_element_type=jnp.float32) + jnp.concatenate(
        [shifts[1], blank, shifts[2]]
    )
    joined = joined.astype(jnp.bfloat16)
    query = joined[:, :width].reshape(seqs, local, HEADS, HEAD_DIM)
    local_pairs = joined[:, width:].reshape(seqs, local, 2 * width)
    all_pairs = lax.all_gather(local_pairs, "seq", axis=1, tiled=True)

    def attend_one(member):
        return attend_forward(member[0], member[1], offset)

    attended, logsum = lax.map(attend_one, (query, all_pairs))
    attended = attended.reshape(seqs * local, width)
    middle = rows_in + (jnp.dot(attended, outproj, preferred_element_type=jnp.float32) + shifts[3])
    second = layer_norm(middle, gains[1], shifts[4]).astype(jnp.bfloat16)
    inner = jnp.dot(second, expand, preferred_element_type=jnp.float32) + shifts[5:9].reshape(-1)
    active = smooth_gate(inner).astype(jnp.bfloat16)
    output = middle + (jnp.dot(active, contract, preferred_element_type=jnp.float32) + shifts[9])
    saved = (rows_in, normed, query, all_pairs, logsum, attended, middle, second, inner, active)
    return (output.reshape(seqs, local, width), saved)


def backward_layer(grad, saved, weights, gains, shifts, offset):
    inproj, outproj, expand, contract = weights
    rows_in, normed, query, pairs_saved, logsum, attended, middle, second, inner, active = saved
    seqs, local = (query.shape[0], query.shape[1])
    width = rows_in.shape[1]
    grad_low = grad.astype(jnp.bfloat16)
    bias_contract = jnp.sum(grad_low, axis=0, dtype=jnp.float32)
    grad_contract = reduce_weight(active, grad_low)
    grad_active = lax.dot_general(
        grad_low, contract, CONTRACT_LAST, preferred_element_type=jnp.float32
    )
    gate_pull = jax.vjp(smooth_gate, inner)[1]
    grad_inner = gate_pull(grad_active)[0].astype(jnp.bfloat16)
    bias_expand = jnp.sum(grad_inner, axis=0, dtype=jnp.float32)
    grad_expand = reduce_weight(second, grad_inner)
    grad_second = lax.dot_general(
        grad_inner, expand, CONTRACT_LAST, preferred_element_type=jnp.float32
    )
    norm_pull = jax.vjp(layer_norm, middle, gains[1], shifts[4])[1]
    grad_middle_norm, gain_two, shift_two = norm_pull(grad_second)
    grad_middle = grad + grad_middle_norm
    branch_low = grad_middle.astype(jnp.bfloat16)
    bias_outproj = jnp.sum(branch_low, axis=0, dtype=jnp.float32)
    grad_outproj = reduce_weight(attended, branch_low)
    grad_attended = lax.dot_general(
        branch_low, outproj, CONTRACT_LAST, preferred_element_type=jnp.float32
    )
    grad_attended = grad_attended.astype(jnp.bfloat16).reshape(seqs, local, width)

    def attend_back(member):
        return attend_backward(member[0], member[1], member[2], member[3], offset)

    grad_query, grad_pairs = lax.map(attend_back, (query, pairs_saved, logsum, grad_attended))
    grad_pairs = lax.psum_scatter(grad_pairs, "seq", scatter_dimension=1, tiled=True)
    grad_joined = jnp.concatenate(
        [grad_query.reshape(seqs * local, width), grad_pairs.reshape(seqs * local, 2 * width)],
        axis=1,
    )
    grad_joined = grad_joined.astype(jnp.bfloat16)
    bias_query = jnp.sum(grad_joined[:, :width], axis=0, dtype=jnp.float32)
    bias_value = jnp.sum(grad_joined[:, 2 * width :], axis=0, dtype=jnp.float32)
    grad_inproj = reduce_weight(normed, grad_joined)
    grad_normed = lax.dot_general(
        grad_joined, inproj, CONTRACT_LAST, preferred_element_type=jnp.float32
    )
    first_pull = jax.vjp(layer_norm, rows_in, gains[0], shifts[0])[1]
    grad_rows, gain_one, shift_one = first_pull(grad_normed)
    grad_out = grad_middle + grad_rows
    gain_grads = jnp.stack([gain_one, gain_two])
    head_rows = jnp.stack([shift_one, bias_query, bias_value, bias_outproj, shift_two])
    shift_grads = jnp.concatenate(
        [head_rows, bias_expand.reshape(4, width), bias_contract[None]], axis=0
    )
    return (
        grad_out,
        (grad_inproj, grad_outproj, grad_expand, grad_contract),
        gain_grads,
        shift_grads,
    )


def adam(weight, first, second, grad, rate, decay):
    momentum = BETA_ONE * first + (1.0 - BETA_ONE) * grad
    variance = BETA_TWO * second + (1.0 - BETA_TWO) * grad * grad
    corrected = momentum / (1.0 - BETA_ONE**STEP)
    scaled = jnp.sqrt(variance / (1.0 - BETA_TWO**STEP))
    updated = weight - rate * (corrected / (scaled + ADAM_EPS) + decay * weight)
    return (momentum, variance, updated)


def body(
    tokens,
    cotangent,
    weight_inproj,
    first_inproj,
    second_inproj,
    weight_outproj,
    first_outproj,
    second_outproj,
    weight_expand,
    first_expand,
    second_expand,
    weight_contract,
    first_contract,
    second_contract,
    gain_values,
    first_gains,
    second_gains,
    bias_values,
    first_biases,
    second_biases,
):
    current = tokens.astype(jnp.float32)
    layers = weight_inproj.shape[0]
    width = tokens.shape[2]
    offset = lax.axis_index("seq") * tokens.shape[1]
    weights = None
    index = 0
    weights = fetch_layer(
        weight_inproj[index], weight_outproj[index], weight_expand[index], weight_contract[index]
    )
    current, saved = forward_layer(current, weights, gain_values[index], bias_values[index], offset)
    stored = [saved]
    grad = cotangent.astype(jnp.float32).reshape(-1, width)
    matrix_grads = [None] * layers
    gain_list = [None] * layers
    shift_list = [None] * layers
    for index in reversed(range(layers)):
        grad, matrices, gain_grad, shift_grad = backward_layer(
            grad, stored[index], weights, gain_values[index], bias_values[index], offset
        )
        matrix_grads[index] = matrices
        gain_list[index] = gain_grad
        shift_list[index] = shift_grad
    gain_total, shift_total = lax.psum((jnp.stack(gain_list), jnp.stack(shift_list)), ("dp", "seq"))
    inproj_grad = jnp.stack([member[0] for member in matrix_grads])
    outproj_grad = jnp.stack([member[1] for member in matrix_grads])
    expand_grad = jnp.stack([member[2] for member in matrix_grads])
    contract_grad = jnp.stack([member[3] for member in matrix_grads])
    inproj_new = adam(
        weight_inproj, first_inproj, second_inproj, inproj_grad, MATRIX_RATE, MATRIX_DECAY
    )
    outproj_new = adam(
        weight_outproj, first_outproj, second_outproj, outproj_grad, MATRIX_RATE, MATRIX_DECAY
    )
    expand_new = adam(
        weight_expand, first_expand, second_expand, expand_grad, MATRIX_RATE, MATRIX_DECAY
    )
    contract_new = adam(
        weight_contract, first_contract, second_contract, contract_grad, MATRIX_RATE, MATRIX_DECAY
    )
    gains_new = adam(gain_values, first_gains, second_gains, gain_total, VECTOR_RATE, 0.0)
    biases_new = adam(bias_values, first_biases, second_biases, shift_total, VECTOR_RATE, 0.0)
    return (
        current,
        grad.reshape(tokens.shape),
        inproj_grad,
        inproj_new[0],
        inproj_new[1],
        inproj_new[2],
        outproj_grad,
        outproj_new[0],
        outproj_new[1],
        outproj_new[2],
        expand_grad,
        expand_new[0],
        expand_new[1],
        expand_new[2],
        contract_grad,
        contract_new[0],
        contract_new[1],
        contract_new[2],
        gain_total,
        gains_new[0],
        gains_new[1],
        gains_new[2],
        shift_total,
        biases_new[0],
        biases_new[1],
        biases_new[2],
    )


def solution(mesh):
    return jax.shard_map(
        body,
        mesh=mesh,
        in_specs=(
            P("dp", "seq", None),
            P("dp", "seq", None),
            P(None, "dp", "seq"),
            P(None, "dp", "seq"),
            P(None, "dp", "seq"),
            P(None, "dp", "seq"),
            P(None, "dp", "seq"),
            P(None, "dp", "seq"),
            P(None, "dp", "seq"),
            P(None, "dp", "seq"),
            P(None, "dp", "seq"),
            P(None, "dp", "seq"),
            P(None, "dp", "seq"),
            P(None, "dp", "seq"),
            P(),
            P(),
            P(),
            P(),
            P(),
            P(),
        ),
        out_specs=(
            P("dp", "seq", None),
            P("dp", "seq", None),
            P(None, "dp", "seq"),
            P(None, "dp", "seq"),
            P(None, "dp", "seq"),
            P(None, "dp", "seq"),
            P(None, "dp", "seq"),
            P(None, "dp", "seq"),
            P(None, "dp", "seq"),
            P(None, "dp", "seq"),
            P(None, "dp", "seq"),
            P(None, "dp", "seq"),
            P(None, "dp", "seq"),
            P(None, "dp", "seq"),
            P(None, "dp", "seq"),
            P(None, "dp", "seq"),
            P(None, "dp", "seq"),
            P(None, "dp", "seq"),
            P(),
            P(),
            P(),
            P(),
            P(),
            P(),
            P(),
            P(),
        ),
        check_vma=False,
    )
```

profile of v0, /device:TPU:0, one launch (start us, length us, event | category | flops | bytes accessed | tf_op | source)
XLA Modules:
  0.0 1956.5 jit_solution(13591825126858930315)
XLA Ops:
  9.2 34.1 %all-gather.18.cloned.1.call-done = bf16[1,1280,960]{2,1,0:T(8,128)(2,1)} async-done(((bf16[1,160,960]{2,1,0:T(8,128)(2,1)}), bf16[1,1280,960]{2,1,0:T(8,128)(2,1)}) %all-gather.18.cloned.1.call-update) | async-done | bytes 2457616 | tf_op jit(solution)/shard_map/all_gather | solution.py:38
  51.1 169.9 %all-gather.20.cloned.1.call-done = bf16[1,1280,3840]{1,2,0:T(8,128)(2,1)} async-done(((bf16[1,1280,960]{1,2,0:T(8,128)(2,1)}), bf16[1,1280,3840]{1,2,0:T(8,128)(2,1)}) %all-gather.20.cloned.1.call-update) | async-done | bytes 9830416 | tf_op jit(solution)/shard_map/all_gather | solution.py:44
  230.3 12.6 all-gather.3
  244.2 13.1 all-gather.26.cloned.1.call-done
  257.4 35.1 %all-gather.30.cloned.1.call-done = bf16[1,5120,320]{1,2,0:T(8,128)(2,1)} async-done(((bf16[1,640,320]{1,2,0:T(8,128)(2,1)}), bf16[1,5120,320]{1,2,0:T(8,128)(2,1)}) %all-gather.30.cloned.1.call-update) | async-done | bytes 3276816 | tf_op jit(solution)/shard_map/all_gather | solution.py:41
  293.7 98.9 %all-gather.22.cloned.1.call-done = bf16[1024,2560]{1,0:T(8,128)(2,1)} async-done(((bf16[256,2560]{1,0:T(8,128)(2,1)}), bf16[1024,2560]{1,0:T(8,128)(2,1)}) %all-gather.22.cloned.1.call-update) | async-done | bytes 5242896 | tf_op jit(solution)/shard_map/all_gather | solution.py:129
  428.4 30.3 %all-gather.24.cloned.1.call-done = bf16[1,1280,1280]{1,2,0:T(8,128)(2,1)} async-done(((bf16[1,1280,320]{1,2,0:T(8,128)(2,1)}), bf16[1,1280,1280]{1,2,0:T(8,128)(2,1)}) %all-gather.24.cloned.1.call-update) | async-done | bytes 3276816 | tf_op jit(solution)/shard_map/all_gather | solution.py:45
  463.3 222.4 %all-gather.28.cloned.1.call-done = bf16[1,1280,5120]{2,1,0:T(8,128)(2,1)} async-done(((bf16[1,1280,1280]{2,1,0:T(8,128)(2,1)}), bf16[1,1280,5120]{2,1,0:T(8,128)(2,1)}) %all-gather.28.cloned.1.call-update) | async-done | bytes 13107216 | tf_op jit(solution)/shard_map/all_gather | solution.py:46
  697.1 215.1 %all-gather.32.cloned.1.call-done = bf16[1,5120,1280]{1,2,0:T(8,128)(2,1)} async-done(((bf16[1,5120,320]{1,2,0:T(8,128)(2,1)}), bf16[1,5120,1280]{1,2,0:T(8,128)(2,1)}) %all-gather.32.cloned.1.call-update) | async-done | bytes 13107216 | tf_op jit(solution)/shard_map/all_gather | solution.py:47
  939.4 13.0 fusion.47
  952.4 13.4 multiply_reduce_fusion
  965.8 14.3 multiply_convert_fusion
  1002.2 16.3 fusion.81
  1019.8 12.4 fusion.95
  1041.6 130.4 %reduce-scatter.16.cloned.1.call-done = f32[1,256,2560]{1,2,0:T(8,128)} async-done(((f32[1,1024,2560]{1,2,0:T(8,128)}), f32[1,256,2560]{1,2,0:T(8,128)}) %reduce-scatter.16.cloned.1.call-update) | async-done | bytes 2621456 | tf_op jit(solution)/shard_map/reduce_scatter | solution.py:178
  1182.7 56.7 %reduce-scatter.20.cloned.1.call-done = f32[160,1280]{1,0:T(8,128)} async-done(((f32[1280,1280]{1,0:T(8,128)}), f32[160,1280]{1,0:T(8,128)}) %reduce-scatter.20.cloned.1.call-update) | async-done | bytes 819216 | tf_op jit(solution)/shard_map/reduce_scatter | solution.py:53
  1242.1 163.8 %reduce-scatter.26.cloned.1.call-done = f32[640,1280]{1,0:T(8,128)} async-done(((f32[5120,1280]{1,0:T(8,128)}), f32[640,1280]{1,0:T(8,128)}) %reduce-scatter.26.cloned.1.call-update) | async-done | bytes 3276816 | tf_op jit(solution)/shard_map/reduce_scatter | solution.py:53
  1410.6 161.8 %reduce-scatter.22.cloned.1.call-done = f32[160,5120]{1,0:T(8,128)} async-done(((f32[1280,5120]{1,0:T(8,128)}), f32[160,5120]{1,0:T(8,128)}) %reduce-scatter.22.cloned.1.call-update) | async-done | bytes 3276816 | tf_op jit(solution)/shard_map/reduce_scatter | solution.py:53
  1579.7 126.4 %reduce-scatter.18.cloned.1.call-done = f32[160,3840]{1,0:T(8,128)} async-done(((f32[1280,3840]{1,0:T(8,128)}), f32[160,3840]{1,0:T(8,128)}) %reduce-scatter.18.cloned.1.call-update) | async-done | bytes 2457616 | tf_op jit(solution)/shard_map/reduce_scatter | solution.py:53
  1711.6 12.3 fusion.51
  1726.6 13.5 reduce-scatter.30.cloned.1.call-done
  1753.8 45.6 %all-reduce = (f32[1,2,1280]{2,1,0:T(2,128)S(1)}, f32[1,10,1280]{2,0,1:T(1,128)S(1)}) all-reduce(f32[1,2,1280]{2,1,0:T(2,128)S(1)} %maximum_bitcast_fusion.1, f32[1,10,1280]{2,0,1:T(1,128)S(1)} %stack.43), channel_id=1, replica_groups=mesh['dp'=8,'seq'=4] {'dp','seq'}, use_global_device_ids=true, to_apply=%region_22.23 | all-reduce | flops 15360 | bytes 122880 | tf_op jit(solution)/shard_map/psum | solution.py:259
  1817.0 52.8 %reduce-scatter.24.cloned.1.call-done = f32[160,1280]{1,0:T(8,128)} async-done(((f32[160,5120]{1,0:T(8,128)}), f32[160,1280]{1,0:T(8,128)}) %reduce-scatter.24.cloned.1.call-update) | async-done | bytes 819216 | tf_op jit(solution)/shard_map/reduce_scatter | solution.py:59
  1873.0 71.9 %reduce-scatter.28.cloned.1.call-done = f32[960,160]{1,0:T(8,128)} async-done(((f32[3840,160]{1,0:T(8,128)}), f32[960,160]{1,0:T(8,128)}) %reduce-scatter.28.cloned.1.call-update) | async-done | bytes 614416
  (245 shorter events, 205.3 us)
Async XLA Ops:
  7.2 36.1 %all-gather.18.cloned.1.call-start = ((), (), s32[]{:S(2)}) async-start(), calls=%async_computation.15 | async-start | bytes 2949120 | tf_op jit(solution)/shard_map/all_gather | solution.py:38
  9.1 211.9 %all-gather.20.cloned.1.call-start = ((), (), s32[]{:S(2)}) async-start(), calls=%async_computation.16 | async-start | bytes 12288000 | tf_op jit(solution)/shard_map/all_gather | solution.py:44
  47.7 209.6 %all-gather.26.cloned.1.call-start = ((), (), s32[]{:S(2)}) async-start(), calls=%async_computation.19 | async-start | bytes 3686400 | tf_op jit(solution)/shard_map/all_gather | solution.py:40
  48.6 243.9 %all-gather.30.cloned.1.call-start = ((), (), s32[]{:S(2)}) async-start(), calls=%async_computation.21 | async-start | bytes 3686400 | tf_op jit(solution)/shard_map/all_gather | solution.py:41
  49.8 342.8 %all-gather.22.cloned.1.call-start = ((), (), s32[]{:S(2)}) async-start(), calls=%async_computation.17 | async-start | bytes 6553600 | tf_op jit(solution)/shard_map/all_gather | solution.py:129
  50.5 177.2 %copy-start.37 = (f32[1280]{0:T(1024)}, f32[1280]{0:T(1024)S(1)}, u32[]{:S(2)}) copy-start(f32[1280]{0:T(1024)S(1)} %get-tuple-element.183) | copy-start | bytes 15364
  50.6 170.5 %copy-start.33 = (f32[1280]{0:T(1024)}, f32[1280]{0:T(1024)S(1)}, u32[]{:S(2)}) copy-start(f32[1280]{0:T(1024)S(1)} %get-tuple-element.186) | copy-start | bytes 15364
  50.8 176.9 %copy-start.42 = (f32[256]{0:T(256)}, f32[256]{0:T(256)S(1)}, u32[]{:S(2)}) copy-start(f32[256]{0:T(256)S(1)} %broadcast_multiply_fusion.2) | copy-start | bytes 3076
  51.1 176.6 %copy-start.56 = (f32[256]{0:T(256)}, f32[256]{0:T(256)S(1)}, u32[]{:S(2)}) copy-start(f32[256]{0:T(256)S(1)} %fusion.71) | copy-start | bytes 3076
  51.1 176.6 %copy-start.46 = (f32[256]{0:T(256)}, f32[256]{0:T(256)S(1)}, u32[]{:S(2)}) copy-start(f32[256]{0:T(256)S(1)} %fusion.88) | copy-start | bytes 3076
  230.2 228.5 %all-gather.24.cloned.1.call-start = ((), (), s32[]{:S(2)}) async-start(), calls=%async_computation.18 | async-start | bytes 4096000 | tf_op jit(solution)/shard_map/all_gather | solution.py:45
  244.1 441.5 %all-gather.28.cloned.1.call-start = ((), (), s32[]{:S(2)}) async-start(), calls=%async_computation.20 | async-start | bytes 16384000 | tf_op jit(solution)/shard_map/all_gather | solution.py:46
  257.4 654.9 %all-gather.32.cloned.1.call-start = ((), (), s32[]{:S(2)}) async-start(), calls=%async_computation.22 | async-start | bytes 16384000 | tf_op jit(solution)/shard_map/all_gather | solution.py:47
  292.5 879.5 %reduce-scatter.16.cloned.1.call-start = ((), (), s32[]{:S(2)}) async-start(), calls=%async_computation.9 | async-start | bytes 13107200 | tf_op jit(solution)/shard_map/reduce_scatter | solution.py:178
  458.7 227.0 %slice-start.1 = ((f32[1,10,1280]{2,0,1:T(1,128)}), f32[1,4,1280]{2,0,1:T(1,128)S(1)}, s32[]{:S(2)}) async-start(f32[1,10,1280]{2,0,1:T(1,128)} %param.37), calls=%async_computation.27 | async-start | bytes 40960 | tf_op jit(solution)/shard_map/slice | solution.py:138
  995.7 243.7 %reduce-scatter.20.cloned.1.call-start = ((), (), s32[]{:S(2)}) async-start(), calls=%async_computation.11 | async-start | bytes 7372800 | tf_op jit(solution)/shard_map/reduce_scatter | solution.py:53
  1001.1 404.8 %reduce-scatter.26.cloned.1.call-start = ((), (), s32[]{:S(2)}) async-start(), calls=%async_computation.14 | async-start | bytes 29491200 | tf_op jit(solution)/shard_map/reduce_scatter | solution.py:53
  1018.5 553.8 %reduce-scatter.22.cloned.1.call-start = ((), (), s32[]{:S(2)}) async-start(), calls=%async_computation.12 | async-start | bytes 29491200 | tf_op jit(solution)/shard_map/reduce_scatter | solution.py:53
  1032.3 673.8 %reduce-scatter.18.cloned.1.call-start = ((), (), s32[]{:S(2)}) async-start(), calls=%async_computation.10 | async-start | bytes 22118400 | tf_op jit(solution)/shard_map/reduce_scatter | solution.py:53
  1041.6 132.4 %copy-start.47 = (f32[256]{0:T(256)S(1)}, f32[256]{0:T(256)}, u32[]{:S(2)}) copy-start(f32[256]{0:T(256)} %copy-done.46) | copy-start | bytes 3076
  1182.7 557.5 %reduce-scatter.30.cloned.1.call-start = ((), (), s32[]{:S(2)}) async-start(), calls=%async_computation.24 | async-start | bytes 1638400
  1242.0 562.6 %reduce-scatter.32.cloned.1.call-start = ((), (), s32[]{:S(2)}) async-start(), calls=%async_computation.25 | async-start | bytes 4096000
  1410.5 459.3 %reduce-scatter.24.cloned.1.call-start = ((), (), s32[]{:S(2)}) async-start(), calls=%async_computation.13 | async-start | bytes 4096000 | tf_op jit(solution)/shard_map/reduce_scatter | solution.py:59
  1572.3 372.5 %reduce-scatter.28.cloned.1.call-start = ((), (), s32[]{:S(2)}) async-start(), calls=%async_computation.23 | async-start | bytes 4915200
  (57 other events, 1343.5 us)
Sparse Core Ops, SparseCore 0:
  10.5 32.8 all-gather.17
  47.8 173.1 all-gather.19
  223.5 33.7 all-gather.25
  259.6 32.8 all-gather.29
  294.5 98.0 all-gather.21
  394.6 64.0 all-gather.23
  460.2 225.3 all-gather.27
  687.2 224.9 all-gather.31
  995.8 176.1 reduce-scatter.15
  1175.3 64.0 reduce-scatter.19
  1243.6 162.3 reduce-scatter.25
  1409.9 162.3 reduce-scatter.21
  1576.4 129.5 reduce-scatter.17
  1708.9 31.1 reduce-scatter.29
  1742.4 62.1 reduce-scatter.31
  1807.5 62.3 reduce-scatter.23
  1872.1 72.7 reduce-scatter.27
where the time goes:
time: 1960 us
  waiting for transfers between devices  1600 us (82%)
  matrix products  159 us (8%)
  local copies, waits for them, and re-layouts  71.6 us (4%)
  blocking collectives  58.1 us (3%)
  other arithmetic  52.1 us (3%)
    reduce_scatter x4, waiting for transfers between devices, reduce_weight(): lax.psum_scatter(lax.dot_general(left, right, CONTRACT_FIRST, preferred_e...  509 us
    all_gather x1, waiting for transfers between devices, fetch_layer(): lax.all_gather(lengthened[2], 'seq', axis=1, tiled=True)  222 us
    all_gather x1, waiting for transfers between devices, fetch_layer(): lax.all_gather(lengthened[3], 'seq', axis=1, tiled=True)  215 us
    all_gather x1, waiting for transfers between devices, fetch_layer(): lax.all_gather(lengthened[0], 'seq', axis=1, tiled=True)  170 us
    reduce_scatter x1, waiting for transfers between devices, backward_layer(): lax.psum_scatter(grad_pairs, 'seq', scatter_dimension=1, tiled=True)  130 us
    all_gather x1, waiting for transfers between devices, forward_layer(): all_pairs = lax.all_gather(local_pairs, 'seq', axis=1, tiled=True)  98.9 us
    unnamed x20, waiting for transfers between devices  89.1 us
    reduce_scatter x1, waiting for transfers between devices, reduce_weight(): return lax.psum_scatter(summed_rows, 'seq', scatter_dimension=1, tiled=True)  52.8 us
  transfers between devices with their start and end apart: 17, of which 17 were waited for; matrix products, arithmetic and copies ran while one was open for 9% of the time, Pallas kernels for 0%

commit v1 on v0

v1 whole, which is shorter than its diff:
```python
import functools

import jax
import jax.numpy as jnp
from jax import lax
from jax.experimental import pallas as pl
from jax.experimental.pallas import tpu as pltpu
from jax.sharding import Mesh
from jax.sharding import PartitionSpec as P

HEADS = 20
HEAD_DIM = 64
STEP = 10
LANES = 128
VMEM_LIMIT = 56 * 2**20


NORM_EPS = 1e-05
BETA_ONE = 0.9
BETA_TWO = 0.95
ADAM_EPS = 1e-08
MATRIX_RATE = 0.02
VECTOR_RATE = 0.15
MATRIX_DECAY = 0.1
CONTRACT_LAST = (((1,), (1,)), ((), ()))
CONTRACT_FIRST = (((0,), (0,)), ((), ()))


def layer_norm(values, gain, shift):
    center = values - jnp.mean(values, axis=-1, keepdims=True)
    spread = jnp.mean(center * center, axis=-1, keepdims=True)
    return center * lax.rsqrt(spread + NORM_EPS) * gain + shift


def smooth_gate(values):
    return jax.nn.gelu(values, approximate=True)


def ring_of_chips(chips):
    half = chips // 2
    return list(range(half)) + list(reversed(range(half, chips)))


def chip_hop(value, direction):
    order = ring_of_chips(lax.axis_size("chip"))
    pairs = [
        (chip, order[(spot + direction) % len(order)]) for spot, chip in enumerate(order)
    ]
    return lax.ppermute(value, "chip", pairs)


def core_swap(value):
    return lax.ppermute(value, "core", [(0, 1), (1, 0)])


def seq_turn(value, distance):
    size = lax.axis_size("seq")
    return lax.ppermute(value, "seq", [(spot, (spot + distance) % size) for spot in range(size)])


def chip_at(offset):
    chips = lax.axis_size("chip")
    order = ring_of_chips(chips)
    mine = lax.axis_index("chip")
    table = [0] * chips
    for spot, chip in enumerate(order):
        table[chip] = order[(spot + offset) % chips]
    return jnp.asarray(table, jnp.int32)[mine]


def after(value, *others):
    if not others:
        return value
    return lax.optimization_barrier((value,) + others)[0]


class Queue:
    def __init__(self, depth=2):
        self.depth = depth
        self.items = []

    def gate(self, *values):
        if len(self.items) < self.depth:
            return values
        return lax.optimization_barrier(values + self.items[-self.depth])[: len(values)]

    def push(self, *values):
        self.items.append(tuple(values))

    def last(self, count=1):
        return tuple(value for item in self.items[len(self.items) - count :] for value in item)


def half_rows(rows):
    return -(-rows // 32) * 16


def row_chunks(rows, parts):
    if parts == 1:
        return [(0, rows)]
    first = rows // parts // 16 * 16
    return [(0, first), (first, rows - first)]


def send_turns(shard, distances):
    return {distance: seq_turn(shard, distance) for distance in distances}


def hold(values, *others):
    arrays = lax.optimization_barrier((*values.values(), *others))[: len(values)]
    return dict(zip(values, arrays))


def side_by_side(shard, moved):
    steps = lax.axis_size("seq")
    place = lax.axis_index("seq")
    stacked = jnp.stack([shard] + [moved[distance] for distance in range(1, steps)])
    return jnp.concatenate(
        [
            lax.dynamic_index_in_dim(stacked, lax.rem(place - spot + steps, steps), 0, False)
            for spot in range(steps)
        ],
        axis=1,
    )


class RingGather:
    def __init__(self, queue, block):
        self.queue = queue
        self.pieces = [(0, 0, block)]
        self.ahead = self.behind = block
        self.step = 0

    def advance(self, *others):
        chips = lax.axis_size("chip")
        self.ahead, self.behind = after(self.ahead, *others), after(self.behind, *others)
        self.step += 1
        step = self.step
        if step < chips // 2:
            up, down = self.queue.gate(self.ahead, self.behind)
            self.ahead, self.behind = chip_hop(up, 1), chip_hop(down, -1)
            self.pieces += [(-step, 0, self.ahead), (step, 0, self.behind)]
        else:
            half = half_rows(self.ahead.shape[0])
            up, down = self.queue.gate(self.ahead[:half], self.behind[half:])
            self.ahead, self.behind = chip_hop(up, 1), chip_hop(down, -1)
            self.pieces += [(step, 0, self.ahead), (step, half, self.behind)]
        self.queue.push(self.ahead, self.behind)


    def hold(self, *others):
        arrays = [piece for _, _, piece in self.pieces]
        arrays = lax.optimization_barrier((*arrays, *others))[: len(arrays)]
        self.pieces = [
            (offset, shift, piece)
            for (offset, shift, _), piece in zip(self.pieces, arrays)
        ]


    def hold_tail(self, count, *others):
        kept = self.pieces[:-count]
        self.pieces = self.pieces[-count:]
        self.hold(*others)
        self.pieces = kept + self.pieces


class RingReduce:
    def __init__(self, queue, block):
        self.queue = queue
        self.block = block
        self.step = lax.axis_size("chip") // 2
        self.ahead = self.behind = None
        self.halves = False

    def hold(self, *others):
        self.ahead, self.behind = after(self.ahead, *others), after(self.behind, *others)

    def arrived(self):
        ahead, behind = self.ahead.astype(jnp.float32), self.behind.astype(jnp.float32)
        if self.halves:
            return (
                jnp.concatenate([ahead, jnp.zeros_like(behind)]),
                jnp.concatenate([jnp.zeros_like(ahead), behind]),
            )
        return ahead, behind

    def advance(self, *others):
        if self.ahead is None:
            opposite = self.block(self.step)
            half = half_rows(opposite.shape[0])
            up, down = opposite[:half], opposite[half:]
            self.halves = True
        else:
            ahead, behind = self.arrived()
            up = (self.block(self.step).astype(jnp.float32) + ahead).astype(jnp.bfloat16)
            down = (self.block(-self.step).astype(jnp.float32) + behind).astype(jnp.bfloat16)
            self.halves = False
        up, down = self.queue.gate(after(up, *others), after(down, *others))
        self.ahead, self.behind = chip_hop(up, 1), chip_hop(down, -1)
        self.queue.push(self.ahead, self.behind)
        self.step -= 1

    def total(self):
        ahead, behind = self.arrived()
        return self.block(0).astype(jnp.float32) + ahead + behind


def advance_all(*rings):
    for _ in range(lax.axis_size("chip") // 2):
        for ring in rings:
            ring.advance()


def whole_vmem():
    return pl.BlockSpec(memory_space=pltpu.VMEM)


def whole_any():
    return pl.BlockSpec(memory_space=pl.ANY)


def place_kernel(plan, starts, *refs):
    sources, target, sems = refs[:-2], refs[-2], refs[-1]
    copies = []
    for spot, (which, first, rows) in enumerate(plan):
        source = sources[which].at[pl.ds(first, rows), :]
        place = pl.multiple_of(starts[spot], 16)
        copies.append(
            pltpu.make_async_copy(source, target.at[pl.ds(place, rows), :], sems.at[spot])
        )
    for copy in copies:
        copy.start()
    for copy in copies:
        copy.wait()


def put_together(rows, arrays, moves):
    starts = jnp.stack([jnp.asarray(move[3], jnp.int32) for move in moves])
    plan = [move[:3] for move in moves]
    cols = arrays[0].shape[1]
    moved = 2 * rows * cols
    return pl.pallas_call(
        functools.partial(place_kernel, plan),
        out_shape=jax.ShapeDtypeStruct((rows, cols), arrays[0].dtype),
        in_specs=[pl.BlockSpec(memory_space=pltpu.SMEM)] + [whole_any()] * len(arrays),
        out_specs=whole_vmem(),
        scratch_shapes=[pltpu.SemaphoreType.DMA((len(moves),))],
        compiler_params=pltpu.CompilerParams(vmem_limit_bytes=VMEM_LIMIT),
        cost_estimate=pl.CostEstimate(flops=0, bytes_accessed=2 * moved, transcendentals=0),
    )(starts, *arrays)


def rows_of_core(gather, rows):
    arrays = [piece for _, _, piece in gather.pieces]
    moves = [
        (spot, 0, piece.shape[0], chip_at(offset) * rows + shift)
        for spot, (offset, shift, piece) in enumerate(gather.pieces)
    ]
    return put_together(lax.axis_size("chip") * rows, arrays, moves)


def rows_of_both(gather, rows, groups):
    core = lax.axis_index("core")
    arrays, moves = [], []
    taken = 0
    for size in groups:
        pieces = gather.pieces[taken : taken + size]
        taken += size
        block = jnp.concatenate([piece for _, _, piece in pieces])
        if arrays:
            block = after(block, arrays[-1])
        arrays += [block, core_swap(block)]
        first = 0
        for offset, shift, piece in pieces:
            count = piece.shape[0]
            chip = chip_at(offset)
            moves.append((len(arrays) - 2, first, count, (2 * chip + core) * rows + shift))
            moves.append((len(arrays) - 1, first, count, (2 * chip + 1 - core) * rows + shift))
            first += count
    return put_together(lax.axis_size("chip") * 2 * rows, arrays, moves)


def mix_cores(packed, chips, low_rows, steps):
    core = lax.axis_index("core")
    both = packed.reshape(chips * low_rows, steps, 2, -1)
    halves = [
        jnp.concatenate([both[:, spot, which] for spot in range(steps)], axis=1)
        .reshape(chips, 1, low_rows, -1)
        for which in range(2)
    ]
    mine = jnp.concatenate(halves, axis=1).reshape(chips, 1, 2 * low_rows, -1)
    theirs = core_swap(mine)
    first = jnp.where(core == 0, mine, theirs)
    second = jnp.where(core == 0, theirs, mine)
    return jnp.concatenate([first, second], axis=1).reshape(chips * 4 * low_rows, -1)


def split_parts(total):
    steps = lax.axis_size("seq")
    place = lax.axis_index("seq")
    cols = total.shape[1] // steps
    low = total.astype(jnp.bfloat16)
    parts = jnp.stack([low[:, spot * cols : (spot + 1) * cols] for spot in range(steps)])
    return [
        lax.dynamic_index_in_dim(parts, lax.rem(place + distance, steps), 0, False)
        for distance in range(steps)
    ]


def send_parts(parts, distances, moved):
    for distance in distances:
        moved[distance] = seq_turn(parts[distance], distance)


def part_sum(parts, moved):
    answer = parts[0].astype(jnp.float32)
    for part in moved.values():
        answer = answer + part.astype(jnp.float32)
    return answer


def product_rows(left, right):
    whole = lax.dot_general(left, right, CONTRACT_FIRST, preferred_element_type=jnp.float32)
    return whole.astype(jnp.bfloat16)


def sum_over_seq(total):
    steps = lax.axis_size("seq")
    cols = total.shape[1] // steps
    parts = jnp.stack([total[:, spot * cols : (spot + 1) * cols] for spot in range(steps)])
    return lax.psum_scatter(parts, "seq", scatter_dimension=0, tiled=False)


def start_reduce(queue, whole, rows, parts):
    def chunk(first, count):
        def block(offset):
            return lax.dynamic_slice_in_dim(whole, chip_at(offset) * rows + first, count, 0)

        return RingReduce(queue, block)

    return [chunk(first, count) for first, count in row_chunks(rows, parts)]


def own_core_columns(values, core):
    chips = lax.axis_size("chip")
    rows = values.shape[1] // (2 * chips)
    halves = []
    for which in range(2):
        halves.append(
            jnp.concatenate(
                [values[:, (2 * chip + which) * rows : (2 * chip + which + 1) * rows] for chip in range(chips)],
                axis=1,
            )
        )
    return jnp.where(core == 0, halves[0], halves[1])


def both_tokens(values):
    return jnp.concatenate([values, core_swap(values)])


def both_left(values):
    core = lax.axis_index("core")
    mine = own_core_columns(values, core)
    theirs = own_core_columns(values, 1 - core)
    return jnp.concatenate([mine, core_swap(theirs)])


def total_along(value, axes):
    for axis in axes:
        size = lax.axis_size(axis)
        reach = 1
        while reach < size:
            value = value + lax.ppermute(value, axis, [(spot, spot ^ reach) for spot in range(size)])
            reach *= 2
    return value


def lanes_up(count):
    return -(-count // LANES) * LANES


def split_kernel(steps, parts, each, source, target):
    wide = parts * each
    for spot in range(steps):
        for part in range(parts):
            first = part * HEADS * HEAD_DIM + spot * each
            count = max(0, min(each, HEADS * HEAD_DIM - spot * each))
            if count:
                target[spot, :, part * each : part * each + count] = source[:, first : first + count]
            if count < each:
                target[spot, :, part * each + count : (part + 1) * each] = jnp.zeros(
                    (target.shape[1], each - count), target.dtype
                )
        if wide < target.shape[2]:
            target[spot, :, wide:] = jnp.zeros(
                (target.shape[1], target.shape[2] - wide), target.dtype
            )


def join_kernel(steps, parts, each, source, target):
    for spot in range(steps):
        count = max(0, min(each, HEADS * HEAD_DIM - spot * each))
        for part in range(parts):
            if count:
                first = part * HEADS * HEAD_DIM + spot * each
                target[:, first : first + count] = source[spot, :, part * each : part * each + count]


def move_kernel(kernel, shape, value):
    return pl.pallas_call(
        kernel,
        out_shape=jax.ShapeDtypeStruct(shape, value.dtype),
        in_specs=[whole_vmem()],
        out_specs=whole_vmem(),
        compiler_params=pltpu.CompilerParams(vmem_limit_bytes=VMEM_LIMIT),
        cost_estimate=pl.CostEstimate(
            flops=0, bytes_accessed=4 * value.size, transcendentals=0
        ),
    )(value)


def to_heads(values, parts):
    steps = lax.axis_size("seq")
    each = -(-HEADS // steps) * HEAD_DIM
    tokens = values.shape[0]
    shape = (steps, tokens, lanes_up(parts * each))
    split = move_kernel(functools.partial(split_kernel, steps, parts, each), shape, values)
    return lax.all_to_all(split, "seq", 0, 0)


def from_heads(values, parts):
    steps, tokens, _ = values.shape
    each = -(-HEADS // steps) * HEAD_DIM
    blocks = lax.all_to_all(values, "seq", 0, 0)
    shape = (tokens, parts * HEADS * HEAD_DIM)
    return move_kernel(functools.partial(join_kernel, steps, parts, each), shape, blocks)


def causal_scores(query, keyed, first):
    scores = lax.dot_general(query, keyed, CONTRACT_LAST, preferred_element_type=jnp.float32)
    scores = scores * HEAD_DIM ** (-0.5)
    rowpos = first + lax.broadcasted_iota(jnp.int32, scores.shape, 0)
    colpos = lax.broadcasted_iota(jnp.int32, scores.shape, 1)
    return jnp.where(colpos <= rowpos, scores, -1000000000.0)


def attend_kernel(heads, held, out_ref, log_ref):
    steps, local = held.shape[:2]
    width = heads * HEAD_DIM
    if width < out_ref.shape[2]:
        out_ref[:, :, width:] = jnp.zeros(
            (steps, local, out_ref.shape[2] - width), out_ref.dtype
        )
    for head in range(heads):
        lanes = slice(head * HEAD_DIM, (head + 1) * HEAD_DIM)
        keyed = held[:, :, width + head * HEAD_DIM : width + (head + 1) * HEAD_DIM]
        valued = held[:, :, 2 * width + head * HEAD_DIM : 2 * width + (head + 1) * HEAD_DIM]
        keyed = keyed.reshape(steps * local, HEAD_DIM)
        valued = valued.reshape(steps * local, HEAD_DIM)
        for block in range(steps):
            reach = (block + 1) * local
            query = held[block, :, lanes]
            scores = causal_scores(query, keyed[:reach], block * local)
            topmost = jnp.max(scores, axis=-1, keepdims=True)
            powers = jnp.exp(scores - topmost)
            totals = jnp.sum(powers, axis=-1, keepdims=True)
            probs = (powers * (1.0 / totals)).astype(jnp.bfloat16)
            output = jnp.dot(probs, valued[:reach], preferred_element_type=jnp.float32)
            log_ref[block, :, head : head + 1] = topmost + jnp.log(totals)
            out_ref[block, :, lanes] = output.astype(jnp.bfloat16)


def attend_back_kernel(heads, held, pulled, log_ref, out_ref, key_sum, value_sum):
    steps, local = held.shape[:2]
    width = heads * HEAD_DIM
    if 3 * width < out_ref.shape[2]:
        out_ref[:, :, 3 * width :] = jnp.zeros(
            (steps, local, out_ref.shape[2] - 3 * width), out_ref.dtype
        )
    scale = HEAD_DIM ** (-0.5)
    for head in range(heads):
        lanes = slice(head * HEAD_DIM, (head + 1) * HEAD_DIM)
        key_lanes = slice(width + head * HEAD_DIM, width + (head + 1) * HEAD_DIM)
        value_lanes = slice(2 * width + head * HEAD_DIM, 2 * width + (head + 1) * HEAD_DIM)
        keyed = held[:, :, key_lanes].reshape(steps * local, HEAD_DIM)
        valued = held[:, :, value_lanes].reshape(steps * local, HEAD_DIM)
        for block in reversed(range(steps)):
            reach = (block + 1) * local
            query = held[block, :, lanes]
            pull = pulled[block, :, lanes]
            scores = causal_scores(query, keyed[:reach], block * local)
            probs = jnp.exp(scores - log_ref[block, :, head : head + 1])
            grad_probs = lax.dot_general(
                pull, valued[:reach], CONTRACT_LAST, preferred_element_type=jnp.float32
            )
            inner = jnp.sum(grad_probs * probs, axis=-1, keepdims=True)
            grad_scores = (probs * (grad_probs - inner)).astype(jnp.bfloat16)
            grad_query = jnp.dot(grad_scores, keyed[:reach], preferred_element_type=jnp.float32)
            grad_key = lax.dot_general(
                grad_scores, query, CONTRACT_FIRST, preferred_element_type=jnp.float32
            )
            grad_value = lax.dot_general(
                probs.astype(jnp.bfloat16), pull, CONTRACT_FIRST, preferred_element_type=jnp.float32
            )
            if block == steps - 1:
                key_sum[...] = grad_key
                value_sum[...] = grad_value
            else:
                key_sum[:reach, :] += grad_key
                value_sum[:reach, :] += grad_value
            out_ref[block, :, lanes] = (grad_query * scale).astype(jnp.bfloat16)
        for block in range(steps):
            rows = slice(block * local, (block + 1) * local)
            out_ref[block, :, key_lanes] = (key_sum[rows, :] * scale).astype(jnp.bfloat16)
            out_ref[block, :, value_lanes] = value_sum[rows, :].astype(jnp.bfloat16)


def attend_forward(held):
    steps, local, _ = held.shape
    heads = -(-HEADS // steps)
    width = lanes_up(heads * HEAD_DIM)
    return pl.pallas_call(
        functools.partial(attend_kernel, heads),
        out_shape=(
            jax.ShapeDtypeStruct((steps, local, width), jnp.bfloat16),
            jax.ShapeDtypeStruct((steps, local, LANES), jnp.float32),
        ),
        in_specs=[whole_vmem()],
        out_specs=(whole_vmem(), whole_vmem()),
        compiler_params=pltpu.CompilerParams(vmem_limit_bytes=VMEM_LIMIT),
        cost_estimate=pl.CostEstimate(flops=10**9, bytes_accessed=4 * 10**6, transcendentals=10**6),
    )(held)


def attend_backward(held, pulled, logsum):
    steps, local, triple = held.shape
    heads = -(-HEADS // steps)
    return pl.pallas_call(
        functools.partial(attend_back_kernel, heads),
        out_shape=jax.ShapeDtypeStruct((steps, local, triple), jnp.bfloat16),
        in_specs=[whole_vmem()] * 3,
        out_specs=whole_vmem(),
        scratch_shapes=[
            pltpu.VMEM((steps * local, HEAD_DIM), jnp.float32),
            pltpu.VMEM((steps * local, HEAD_DIM), jnp.float32),
        ],
        compiler_params=pltpu.CompilerParams(vmem_limit_bytes=VMEM_LIMIT),
        cost_estimate=pl.CostEstimate(flops=10**9, bytes_accessed=4 * 10**6, transcendentals=10**6),
    )(held, pulled, logsum)


def layer(tokens, cotangent, shards, gains, shifts):
    chips = lax.axis_size("chip")
    core = lax.axis_index("core")
    steps = lax.axis_size("seq")
    place = lax.axis_index("seq")
    seqs, local, width = tokens.shape
    count = seqs * local
    turns = chips // 2

    inproj, outproj, expand, contract = [shard.astype(jnp.bfloat16) for shard in shards]
    rows, long_rows = inproj.shape[0], contract.shape[0]
    half = expand.shape[1] // 2
    kept = lax.dynamic_slice_in_dim(expand, core * half, half, 1)
    given = core_swap(lax.dynamic_slice_in_dim(expand, (1 - core) * half, half, 1))
    expand = jnp.concatenate(
        [jnp.where(core == 0, kept, given), jnp.where(core == 0, given, kept)]
    )

    rows_in = tokens.astype(jnp.float32).reshape(count, width)
    grad_low = cotangent.reshape(count, width)
    grad = grad_low.astype(jnp.float32)
    normed = layer_norm(rows_in, gains[0], shifts[0]).astype(jnp.bfloat16)

    inproj_moved = send_turns(inproj, range(1, steps))
    inproj_ring = RingGather(Queue(), side_by_side(inproj, inproj_moved))
    inproj_ring.advance(given)
    inproj_first = inproj_ring.queue.last()
    expand = lax.all_gather(after(expand, *inproj_moved.values()), "seq", axis=1, tiled=True)
    contract = lax.all_gather(after(contract, *inproj_moved.values()), "seq", axis=1, tiled=True)
    for _ in range(turns - 1):
        inproj_ring.advance()
    inproj_last = inproj_ring.queue.last()
    expand = lax.all_gather(after(expand, *inproj_last), "chip", axis=0, tiled=True)
    outproj_moved = send_turns(after(outproj, *inproj_moved.values()), range(1, steps))
    pieces = len(inproj_ring.pieces)
    inproj = rows_of_both(inproj_ring, rows, [pieces - 2, 2])

    blank = jnp.zeros_like(shifts[1])
    joined = jnp.dot(normed, inproj, preferred_element_type=jnp.float32) + jnp.concatenate(
        [shifts[1], blank, shifts[2]]
    )
    joined = joined.astype(jnp.bfloat16)
    held = to_heads(joined, 3)
    contract = lax.all_gather(after(contract, joined), "chip", axis=0, tiled=True)
    outproj_ring = RingGather(Queue(), side_by_side(outproj, hold(outproj_moved, joined)))
    outproj_ring.advance()
    outproj_first = outproj_ring.queue.last()
    for _ in range(turns - 1):
        outproj_ring.advance()
    outproj = rows_of_both(outproj_ring, rows, [pieces])
    held = after(held, outproj)
    attended, logsum = attend_forward(held)
    attended = from_heads(attended, 1)
    middle = rows_in + (jnp.dot(attended, outproj, preferred_element_type=jnp.float32) + shifts[3])
    second = layer_norm(middle, gains[1], shifts[4]).astype(jnp.bfloat16)

    second_both = both_tokens(second)
    grad_both = both_tokens(grad_low)
    hidden = shifts[5:9].reshape(steps, 2, -1)
    hidden = lax.dynamic_index_in_dim(hidden, core, 1, False).reshape(-1)
    inner = jnp.dot(second_both, expand, preferred_element_type=jnp.float32) + hidden
    active = smooth_gate(inner).astype(jnp.bfloat16)
    contract_whole = product_rows(active, grad_both)
    contract_total = lax.psum_scatter(contract_whole, "chip", scatter_dimension=0, tiled=True)

    bias_contract = jnp.sum(grad_low, axis=0, dtype=jnp.float32)
    grad_active = lax.dot_general(
        after(grad_both, contract_whole), contract, CONTRACT_LAST, preferred_element_type=jnp.float32
    )
    gate_pull = jax.vjp(smooth_gate, inner)[1]
    grad_inner = gate_pull(grad_active)[0].astype(jnp.bfloat16)
    grad_second = lax.dot_general(
        grad_inner, expand, CONTRACT_LAST, preferred_element_type=jnp.float32
    )
    expand_whole = product_rows(after(second_both, grad_second), grad_inner)
    expand_total = lax.psum_scatter(expand_whole, "chip", scatter_dimension=0, tiled=True)
    bias_expand = jnp.sum(grad_inner, axis=0, dtype=jnp.float32).reshape(steps, 1, -1)
    bias_expand = jnp.where(
        jnp.arange(2)[None, :, None] == core, bias_expand, 0.0
    ).reshape(4, width)
    grad_second = grad_second[:count] + core_swap(grad_second[count:])
    grad_second = after(grad_second, expand_whole)
    norm_pull = jax.vjp(layer_norm, middle, gains[1], shifts[4])[1]
    grad_middle_norm, gain_two, shift_two = norm_pull(grad_second)
    grad_middle = grad + grad_middle_norm
    branch_low = grad_middle.astype(jnp.bfloat16)
    bias_outproj = jnp.sum(branch_low, axis=0, dtype=jnp.float32)
    grad_attended = lax.dot_general(
        branch_low, outproj, CONTRACT_LAST, preferred_element_type=jnp.float32
    ).astype(jnp.bfloat16)
    pulled = to_heads(grad_attended, 1)

    partial = jnp.dot(after(active, grad_attended), contract, preferred_element_type=jnp.float32)
    output = middle + (partial[:count] + core_swap(partial[count:]) + shifts[9])
    outproj_whole = product_rows(both_left(attended), both_tokens(after(branch_low, grad_attended)))
    outproj_queue = Queue(1)
    (outproj_sum,) = start_reduce(outproj_queue, outproj_whole, rows, 1)
    outproj_sum.advance()
    pulled = after(pulled, output, contract_total, *outproj_queue.last())
    grad_heads = attend_backward(held, pulled, logsum)
    outproj_sum.hold(grad_heads)
    for _ in range(turns - 1):
        outproj_sum.advance()
    outproj_last = outproj_queue.last()
    contract_grad = sum_over_seq(after(contract_total, grad_heads))
    outproj_parts = split_parts(outproj_sum.total())
    normed_both = both_left(after(normed, grad_heads))
    grad_joined = after(
        from_heads(grad_heads, 3), expand_total, normed_both, *outproj_parts[1:]
    )
    expand_own = sum_over_seq(after(expand_total, grad_joined))

    joined_both = both_tokens(grad_joined)
    inproj_whole = product_rows(normed_both, joined_both)
    inproj_sums = start_reduce(Queue(2), inproj_whole, rows, 2)
    advance_all(*inproj_sums)
    inproj_items = inproj_sums[0].queue.items
    outproj_moved = {}
    send_parts([after(part, grad_joined) for part in outproj_parts], range(1, steps), outproj_moved)
    inproj_grad = []
    inproj_moved = []
    for part in inproj_sums:
        parts, moved = split_parts(part.total()), {}
        send_parts(parts, range(1, steps), moved)
        inproj_moved += list(moved.values())
        inproj_grad.append(part_sum(parts, moved))
    inproj_grad = jnp.concatenate(inproj_grad)
    outproj_grad = part_sum(outproj_parts, hold(outproj_moved, *inproj_moved[: steps - 1]))
    contract_grad = after(contract_grad, *inproj_moved[: steps - 1]).astype(jnp.float32)
    expand_own = after(expand_own, *inproj_moved[: steps - 1]).astype(jnp.float32)
    kept = lax.dynamic_slice_in_dim(expand_own, core * rows, rows, 0)
    given = core_swap(lax.dynamic_slice_in_dim(expand_own, (1 - core) * rows, rows, 0))
    expand_grad = jnp.concatenate(
        [jnp.where(core == 0, kept, given), jnp.where(core == 0, given, kept)], axis=1
    )

    bias_query = jnp.sum(grad_joined[:, :width], axis=0, dtype=jnp.float32)
    bias_value = jnp.sum(grad_joined[:, 2 * width :], axis=0, dtype=jnp.float32)
    grad_normed = lax.dot_general(
        grad_joined, inproj, CONTRACT_LAST, preferred_element_type=jnp.float32
    )
    first_pull = jax.vjp(layer_norm, rows_in, gains[0], shifts[0])[1]
    grad_rows, gain_one, shift_one = first_pull(grad_normed)
    grad_out = grad_middle + grad_rows
    sums = total_along(
        jnp.concatenate(
            [
                jnp.stack(
                    [gain_one, gain_two, shift_one, bias_query, bias_value, bias_outproj, shift_two]
                ),
                bias_expand,
                bias_contract[None],
            ]
        ),
        ("core", "chip"),
    )
    sums = total_along(after(sums, *inproj_items[0]), ("seq",))
    return (
        output.reshape(tokens.shape),
        grad_out.reshape(tokens.shape),
        (inproj_grad, outproj_grad, expand_grad, contract_grad),
        sums[:2],
        sums[2:],
    )


def adam(weight, first, second, grad, rate, decay):
    momentum = BETA_ONE * first + (1.0 - BETA_ONE) * grad
    variance = BETA_TWO * second + (1.0 - BETA_TWO) * grad * grad
    corrected = momentum / (1.0 - BETA_ONE**STEP)
    scaled = jnp.sqrt(variance / (1.0 - BETA_TWO**STEP))
    updated = weight - rate * (corrected / (scaled + ADAM_EPS) + decay * weight)
    return (momentum, variance, updated)


def body(
    tokens,
    cotangent,
    weight_inproj,
    first_inproj,
    second_inproj,
    weight_outproj,
    first_outproj,
    second_outproj,
    weight_expand,
    first_expand,
    second_expand,
    weight_contract,
    first_contract,
    second_contract,
    gain_values,
    first_gains,
    second_gains,
    bias_values,
    first_biases,
    second_biases,
):
    current, grad, matrices, gain_total, shift_total = layer(
        tokens,
        cotangent,
        (weight_inproj[0], weight_outproj[0], weight_expand[0], weight_contract[0]),
        gain_values[0],
        bias_values[0],
    )
    inproj_grad, outproj_grad, expand_grad, contract_grad = [member[None] for member in matrices]
    gain_total, shift_total = (gain_total[None], shift_total[None])
    inproj_new = adam(
        weight_inproj, first_inproj, second_inproj, inproj_grad, MATRIX_RATE, MATRIX_DECAY
    )
    outproj_new = adam(
        weight_outproj, first_outproj, second_outproj, outproj_grad, MATRIX_RATE, MATRIX_DECAY
    )
    expand_new = adam(
        weight_expand, first_expand, second_expand, expand_grad, MATRIX_RATE, MATRIX_DECAY
    )
    contract_new = adam(
        weight_contract, first_contract, second_contract, contract_grad, MATRIX_RATE, MATRIX_DECAY
    )
    gains_new = adam(gain_values, first_gains, second_gains, gain_total, VECTOR_RATE, 0.0)
    biases_new = adam(bias_values, first_biases, second_biases, shift_total, VECTOR_RATE, 0.0)
    return (
        current,
        grad,
        inproj_grad,
        inproj_new[0],
        inproj_new[1],
        inproj_new[2],
        outproj_grad,
        outproj_new[0],
        outproj_new[1],
        outproj_new[2],
        expand_grad,
        expand_new[0],
        expand_new[1],
        expand_new[2],
        contract_grad,
        contract_new[0],
        contract_new[1],
        contract_new[2],
        gain_total,
        gains_new[0],
        gains_new[1],
        gains_new[2],
        shift_total,
        biases_new[0],
        biases_new[1],
        biases_new[2],
    )


def solution(mesh):
    size, steps = mesh.devices.shape
    mesh = Mesh(mesh.devices.reshape(size // 2, 2, steps), ("chip", "core", "seq"))
    return jax.shard_map(
        body,
        mesh=mesh,
        in_specs=(
            P(("chip", "core"), "seq", None),
            P(("chip", "core"), "seq", None),
            P(None, ("chip", "core"), "seq"),
            P(None, ("chip", "core"), "seq"),
            P(None, ("chip", "core"), "seq"),
            P(None, ("chip", "core"), "seq"),
            P(None, ("chip", "core"), "seq"),
            P(None, ("chip", "core"), "seq"),
            P(None, ("chip", "core"), "seq"),
            P(None, ("chip", "core"), "seq"),
            P(None, ("chip", "core"), "seq"),
            P(None, ("chip", "core"), "seq"),
            P(None, ("chip", "core"), "seq"),
            P(None, ("chip", "core"), "seq"),
            P(),
            P(),
            P(),
            P(),
            P(),
            P(),
        ),
        out_specs=(
            P(("chip", "core"), "seq", None),
            P(("chip", "core"), "seq", None),
            P(None, ("chip", "core"), "seq"),
            P(None, ("chip", "core"), "seq"),
            P(None, ("chip", "core"), "seq"),
            P(None, ("chip", "core"), "seq"),
            P(None, ("chip", "core"), "seq"),
            P(None, ("chip", "core"), "seq"),
            P(None, ("chip", "core"), "seq"),
            P(None, ("chip", "core"), "seq"),
            P(None, ("chip", "core"), "seq"),
            P(None, ("chip", "core"), "seq"),
            P(None, ("chip", "core"), "seq"),
            P(None, ("chip", "core"), "seq"),
            P(None, ("chip", "core"), "seq"),
            P(None, ("chip", "core"), "seq"),
            P(None, ("chip", "core"), "seq"),
            P(None, ("chip", "core"), "seq"),
            P(),
            P(),
            P(),
            P(),
            P(),
            P(),
            P(),
            P(),
        ),
        check_vma=False,
    )
```

time: 1960 us -> 591 us (0.30)
  waiting for transfers between devices: 1600 us -> 233 us
  matrix products: 159 us -> 73.9 us
  starting transfers between devices: 0.91 us -> 63.6 us
  Pallas kernels: 0 us -> 55.3 us
  blocking collectives: 58.1 us -> 24.6 us
    all_gather x8 -> x4, waiting for transfers between devices: 819 us -> 14.6 us  [the longest x1 14.6 us: layer(): lax.all_gather(after(contract, joined), 'chip', axis=0, tiled=True)]
    reduce_scatter x6 -> x4, waiting for transfers between devices: 692 us -> 12.7 us  [the longest x1 7.9 us: layer(): lax.psum_scatter(expand_whole, 'chip', scatter_dimension=0, tiled=True)]
    ppermute x0 -> x53, waiting for transfers between devices: none -> 181 us  [the longest x20 99.5 us: chip_hop(): return lax.ppermute(value, 'chip', pairs)]
    unnamed x20 -> x8, waiting for transfers between devices: 89.1 us -> 0.13 us
    dot_general x18 -> x12, matrix products: 159 us -> 73.9 us  [the longest x4 19.3 us: product_rows(): lax.dot_general(left, right, CONTRACT_FIRST, preferred_element_type=jnp.f...]
    pallas_call x0 -> x8, Pallas kernels: none -> 55.3 us  [the longest x1 18.2 us: attend_backward(): pl.pallas_call(functools.partial(attend_back_kernel, heads), out_shape=ja...]
    ppermute x0 -> x53, starting transfers between devices: none -> 50 us  [the longest x20 24.1 us: chip_hop(): return lax.ppermute(value, 'chip', pairs)]
    psum x1 -> x0, blocking collectives: 45.6 us -> none  [body(): lax.psum((jnp.stack(gain_list), jnp.stack(shift_list)), ('dp', 'seq'))]
  transfers between devices with their start and end apart: 17 -> 64, of which waited for: 17 -> 31; matrix products, arithmetic and copies ran while one was open for 9% -> 28% of each run, Pallas kernels for 0% -> 9%
where the time goes in v1:
time: 591 us; the launch traced here: 583 us
  waiting for transfers between devices  233 us (39%)
  matrix products  73.9 us (13%)
  starting transfers between devices  63.6 us (11%)
  local copies, waits for them, and re-layouts  57 us (10%)
  other arithmetic  55.9 us (9%)
  Pallas kernels  55.3 us (9%)
  blocking collectives  24.6 us (4%)
  between operations  19.9 us (3%)
    ppermute x20, waiting for transfers between devices, chip_hop(): return lax.ppermute(value, 'chip', pairs)  99.5 us
    ppermute x15, waiting for transfers between devices, seq_turn(): lax.ppermute(value, 'seq', [(spot, (spot + distance) % size) for spot in...  62 us
    unnamed x209, local copies, waits for them, and re-layouts  33.3 us
    all_to_all x1, blocking collectives, from_heads(): blocks = lax.all_to_all(values, 'seq', 0, 0)  24.6 us
    ppermute x20, starting transfers between devices, chip_hop(): return lax.ppermute(value, 'chip', pairs)  24.1 us
    ppermute x15, starting transfers between devices, seq_turn(): lax.ppermute(value, 'seq', [(spot, (spot + distance) % size) for spot in...  19.6 us
    dot_general x4, matrix products, product_rows(): lax.dot_general(left, right, CONTRACT_FIRST, preferred_element_type=jnp.f...  19.3 us
    pallas_call x1, Pallas kernels, attend_backward(): pl.pallas_call(functools.partial(attend_back_kernel, heads), out_shape=ja...  18.2 us
  transfers between devices with their start and end apart: 64, of which 31 were waited for; matrix products, arithmetic and copies ran while one was open for 28% of the time, Pallas kernels for 9%

profile of v1, /device:TPU:0, one launch (start us, length us, event | category | flops | bytes accessed | tf_op | source)
XLA Modules:
  0.0 583.0 jit_solution(10669916612585892658)
XLA Ops:
  22.5 20.5 %collective-permute-done.1 = bf16[160,960]{1,0:T(8,128)(2,1)S(1)} collective-permute-done((bf16[160,960]{1,0:T(8,128)(2,1)S(1)}, bf16[160,960]{1,0:T(8,128)(2,1)S(1)}, u32[]{:S(2)}, u32[]{:S(2)}) %collective-permute-start.1) | collective-permute-done | bytes 307232 | tf_op jit(solution)/shard_map/ppermute | solution.py:58
  47.6 26.6 %collective-permute-done.5 = bf16[160,3840]{1,0:T(8,128)(2,1)S(1)} collective-permute-done((bf16[160,3840]{1,0:T(8,128)(2,1)S(1)}, bf16[160,3840]{1,0:T(8,128)(2,1)S(1)}, u32[]{:S(2)}, u32[]{:S(2)}) %collective-permute-start.5) | collective-permute-done | bytes 1228832 | tf_op jit(solution)/shard_map/ppermute | solution.py:49
  77.5 11.7 %collective-permute-done.8 = bf16[80,3840]{1,0:T(8,128)(2,1)} collective-permute-done((bf16[80,3840]{1,0:T(8,128)(2,1)S(1)}, bf16[80,3840]{1,0:T(8,128)(2,1)}, u32[]{:S(2)}, u32[]{:S(2)}) %collective-permute-start.8) | collective-permute-done | bytes 614432 | tf_op jit(solution)/shard_map/ppermute | solution.py:49
  109.7 8.4 %shard_map.593 = bf16[1280,3840]{1,0:T(8,128)(2,1)} custom-call(s32[10]{0:T(128)} %stack.190.starts, bf16[480,3840]{1,0:T(8,128)(2,1)} %copy-done.1, bf16[480,3840]{1,0:T(8,128)(2,1)} %copy-done.20, bf16[160,3840]{1,0:T(8,128)(2,1)} %copy-done.12, bf16[160,3840]{1,0:T(8,128)(2,1)} %copy-done.39), custom_call_target="tpu_custom_call" | custom-call | bytes 19660800 | tf_op jit(solution)/shard_map/pallas_call | solution.py:242
  118.2 7.7 %fusion.7.source = bf16[256,3840]{1,0:T(8,128)(2,1)} fusion(bf16[256,1280]{1,0:T(8,128)(2,1)S(1)} %fusion.20, bf16[1280,3840]{1,0:T(8,128)(2,1)} %shard_map.593, f32[3840]{0:T(1024)S(1)} %pad_maximum_fusion.19), kind=kOutput, calls=%fused_computation.15 | convolution fusion | flops 2518548480 | bytes 12467200 | tf_op jit(solution)/shard_map/dot_general | solution.py:591
  145.9 13.9 %collective-permute-done.13 = bf16[160,1280]{1,0:T(8,128)(2,1)S(1)} collective-permute-done((bf16[160,1280]{1,0:T(8,128)(2,1)S(1)}, bf16[160,1280]{1,0:T(8,128)(2,1)S(1)}, u32[]{:S(2)}, u32[]{:S(2)}) %collective-permute-start.13) | collective-permute-done | bytes 409632 | tf_op jit(solution)/shard_map/ppermute | solution.py:49
  162.3 8.6 %collective-permute-done.15 = bf16[80,1280]{1,0:T(8,128)(2,1)S(1)} collective-permute-done((bf16[80,1280]{1,0:T(8,128)(2,1)S(1)}, bf16[80,1280]{1,0:T(8,128)(2,1)S(1)}, u32[]{:S(2)}, u32[]{:S(2)}) %collective-permute-start.15) | collective-permute-done | bytes 204832 | tf_op jit(solution)/shard_map/ppermute | solution.py:49
  180.6 7.4 %all-to-all-done.held = bf16[4,256,1024]{2,1,0:T(8,128)(2,1)S(1)} async-done(((bf16[4,256,1024]{2,1,0:T(8,128)(2,1)}), bf16[4,256,1024]{2,1,0:T(8,128)(2,1)S(1)}, u32[]{:S(2)}, u32[]{:S(2)}) %all-to-all-start) | async-done | bytes 2097184 | tf_op jit(solution)/shard_map/all_to_all | solution.py:429
  189.4 13.2 %shard_map.596 = (bf16[4,256,384]{2,1,0:T(8,128)(2,1)}, f32[4,256,128]{2,1,0:T(8,128)}) custom-call(bf16[4,256,1024]{2,1,0:T(8,128)(2,1)} %copy-done.2), custom_call_target="tpu_custom_call" | custom-call | flops 1000000000 | bytes 4000000 | tf_op jit(solution)/shard_map/pallas_call | solution.py:523
  202.6 24.6 %all_to_all.20.source = bf16[4,256,384]{2,1,0:T(8,128)(2,1)} all-to-all(bf16[4,256,384]{2,1,0:T(8,128)(2,1)} %get-tuple-element.73), channel_id=1, replica_groups=mesh['chip'=4,'core'=2,'seq'=4] {'seq'}, dimensions={0} | all-to-all | bytes 1572864 | tf_op jit(solution)/shard_map/all_to_all | solution.py:435
  238.7 10.8 %multiply_convert_fusion = (bf16[512,2560]{1,0:T(8,128)(2,1)S(1)}, f32[512,2560]{1,0:T(8,128)}) fusion(f32[2560]{0:T(1024)} %add.604, bf16[1280,2560]{1,0:T(8,128)(2,1)} %all-gather.7.cloned.1.call-done, bf16[256,1280]{1,0:T(8,128)(2,1)} %collective-permute-done.18, bf16[256,1280]{1,0:T(8,128)(2,1)S(1)} %add_convert_fusion), kind=kOutput, calls=%fused_computation.14 | convolution fusion | flops 3371171840 | bytes 15738880 | tf_op jit(solution)/shard_map/dot_general | solution.py:613
  251.0 6.7 %convolution_convert_fusion.1 = bf16[2560,1280]{1,0:T(8,128)(2,1)} fusion(bf16[512,2560]{1,0:T(8,128)(2,1)S(1)} %get-tuple-element.81, bf16[256,1280]{1,0:T(8,128)(2,1)} %collective-permute-done.19, bf16[256,1280]{1,0:T(8,128)(2,1)S(1)} %bitcast.230), kind=kOutput, calls=%fused_computation.1 | convolution fusion | flops 3361341440 | bytes 10485760 | tf_op jit(solution)/shard_map/dot_general | solution.py:323
  262.4 14.6 %all-gather.11.cloned.1.call-done = bf16[2560,1280]{0,1:T(8,128)(2,1)} async-done(((bf16[640,1280]{0,1:T(8,128)(2,1)}), bf16[2560,1280]{0,1:T(8,128)(2,1)}) %all-gather.11.cloned.1.call-update) | async-done | bytes 6553616 | tf_op jit(solution)/shard_map/all_gather | solution.py:596
  277.0 10.0 %convert_reduce_fusion = (f32[2560]{0:T(1024)}, bf16[512,2560]{1,0:T(8,128)(2,1)S(1)}) fusion(f32[512,2560]{1,0:T(8,128)} %get-tuple-element.254, bf16[512,1280]{1,0:T(8,128)(2,1)} %pad_maximum_fusion.5, bf16[2560,1280]{0,1:T(8,128)(2,1)} %all-gather.11.cloned.1.call-done), kind=kOutput, calls=%fused_computation.13 | convolution fusion | flops 3384276480 | bytes 15738880 | tf_op jit(solution)/shard_map/dot_general | solution.py:619
  287.0 8.1 %fusion.68 = f32[512,1280]{1,0:T(8,128)} fusion(bf16[512,2560]{1,0:T(8,128)(2,1)S(1)} %get-tuple-element.156, bf16[1280,2560]{1,0:T(8,128)(2,1)} %all-gather.7.cloned.1.call-done), kind=kOutput, calls=%fused_computation.224 | convolution fusion | flops 3355443200 | bytes 11796480 | tf_op jit(solution)/shard_map/dot_general | solution.py:624
  311.4 6.6 %fusion.69 = f32[512,1280]{1,0:T(8,128)S(1)} fusion(bf16[512,2560]{1,0:T(8,128)(2,1)S(1)} %copy-done.97, bf16[2560,1280]{0,1:T(8,128)(2,1)} %all-gather.11.cloned.1.call-done), kind=kOutput, calls=%fused_computation.225 | convolution fusion | flops 3355443200 | bytes 11796480 | tf_op jit(solution)/shard_map/dot_general | solution.py:645
  339.7 7.1 %collective-permute-done.24 = bf16[80,1280]{1,0:T(8,128)(2,1)S(1)} collective-permute-done((bf16[80,1280]{1,0:T(8,128)(2,1)S(1)}, bf16[80,1280]{1,0:T(8,128)(2,1)S(1)}, u32[]{:S(2)}, u32[]{:S(2)}) %collective-permute-start.24) | collective-permute-done | bytes 204832 | tf_op jit(solution)/shard_map/ppermute | solution.py:49
  356.7 18.2 %shard_map.599 = bf16[4,256,1024]{2,1,0:T(8,128)(2,1)} custom-call(bf16[4,256,1024]{2,1,0:T(8,128)(2,1)} %copy-done.2, bf16[4,256,384]{2,1,0:T(8,128)(2,1)} %all-to-all-done.2.pulled, f32[4,256,128]{2,1,0:T(8,128)} %get-tuple-element.84.log_ref), custom_call_target="tpu_custom_call" | custom-call | flops 1000000000 | bytes 4000000 | tf_op jit(solution)/shard_map/pallas_call | solution.py:539
  399.1 13.1 %collective-permute-done.28 = bf16[160,1280]{1,0:T(8,128)(2,1)} collective-permute-done((bf16[160,1280]{1,0:T(8,128)(2,1)}, bf16[160,1280]{1,0:T(8,128)(2,1)}, u32[]{:S(2)}, u32[]{:S(2)}) %collective-permute-start.28) | collective-permute-done | bytes 409632 | tf_op jit(solution)/shard_map/ppermute | solution.py:49
  414.8 13.3 %all-to-all-done.3.source = bf16[4,256,1024]{2,1,0:T(8,128)(2,1)} async-done(((bf16[4,256,1024]{2,1,0:T(8,128)(2,1)}), bf16[4,256,1024]{2,1,0:T(8,128)(2,1)}, u32[]{:S(2)}, u32[]{:S(2)}) %all-to-all-start.3) | async-done | bytes 2097184 | tf_op jit(solution)/shard_map/all_to_all | solution.py:435
  431.4 7.9 %reduce-scatter.7.cloned.1.call-done = bf16[320,2560]{1,0:T(8,128)(2,1)} async-done(((bf16[1280,2560]{1,0:T(8,128)(2,1)}), bf16[320,2560]{1,0:T(8,128)(2,1)}) %reduce-scatter.7.cloned.1.call-update) | async-done | bytes 1638416 | tf_op jit(solution)/shard_map/reduce_scatter | solution.py:628
  439.3 7.2 %fusion.54 = (f32[1280]{0:T(1024)S(1)}, f32[256]{0:T(256)S(1)}, f32[256,1280]{1,0:T(8,128)S(1)}) fusion(f32[1280]{0:T(1024)S(1)} %get-tuple-element.148, f32[256]{0:T(256)S(1)} %copy-done.76, bf16[1,256,1280]{2,1,0:T(8,128)(2,1)S(1)} %copy-done, bf16[256,3840]{1,0:T(8,128)(2,1)} %shard_map.600, bf16[1280,3840]{1,0:T(8,128)(2,1)} %shard_map.593), kind=kOutput, calls=%fused_computation.219 | convolution fusion | flops 2518546944 | bytes 13774848 | tf_op jit(solution)/shard_map/dot_general | solution.py:691
  517.5 20.0 %collective-permute-done.35 = bf16[80,960]{1,0:T(8,128)(2,1)S(1)} collective-permute-done((bf16[80,960]{1,0:T(8,128)(2,1)S(1)}, bf16[80,960]{1,0:T(8,128)(2,1)S(1)}, u32[]{:S(2)}, u32[]{:S(2)}) %collective-permute-start.35) | collective-permute-done | bytes 153632 | tf_op jit(solution)/shard_map/ppermute | solution.py:58
  565.2 8.2 %collective-permute-done.42 = bf16[80,960]{1,0:T(8,128)(2,1)S(1)} collective-permute-done((bf16[80,960]{1,0:T(8,128)(2,1)S(1)}, bf16[80,960]{1,0:T(8,128)(2,1)S(1)}, u32[]{:S(2)}, u32[]{:S(2)}) %collective-permute-start.42) | collective-permute-done | bytes 153632 | tf_op jit(solution)/shard_map/ppermute | solution.py:58
  (463 shorter events, 268.7 us)
Async XLA Ops:
  7.2 84.3 %all-gather.5.cloned.1.call-start = ((), (), s32[]{:S(2)}) async-start(), calls=%async_computation.8 | async-start | bytes 2048000 | tf_op jit(solution)/shard_map/all_gather | solution.py:580
  14.4 28.6 %collective-permute-start.1 = (bf16[160,960]{1,0:T(8,128)(2,1)S(1)}, bf16[160,960]{1,0:T(8,128)(2,1)S(1)}, u32[]{:S(2)}, u32[]{:S(2)}) collective-permute-start(bf16[160,960]{1,0:T(8,128)(2,1)S(1)} %convert_bitcast_fusion.4), channel_id=1, source_target_pairs={{0,2},{1,3},{2,0},{3,1},{4,6},{5,7},{6,4},{7,5},{8,10},{9,11},{10,... | collective-permute-start | bytes 921608 | tf_op jit(solution)/shard_map/ppermute | solution.py:58
  14.4 28.6 %collective-permute-start = (bf16[160,960]{1,0:T(8,128)(2,1)S(1)}, bf16[160,960]{1,0:T(8,128)(2,1)S(1)}, u32[]{:S(2)}, u32[]{:S(2)}) collective-permute-start(bf16[160,960]{1,0:T(8,128)(2,1)S(1)} %convert_bitcast_fusion.4), channel_id=1, source_target_pairs={{0,1},{1,2},{2,3},{3,0},{4,5},{5,6},{6,7},{7,4},{8,9},{9,10},{10,1... | collective-permute-start | bytes 921608 | tf_op jit(solution)/shard_map/ppermute | solution.py:58
  43.0 82.9 %all-gather.9.cloned.1.call-start = ((), (), s32[]{:S(2)}) async-start(), calls=%async_computation.10 | async-start | bytes 2048000 | tf_op jit(solution)/shard_map/all_gather | solution.py:581
  43.9 194.8 %all-gather.7.cloned.1.call-start = ((), (), s32[]{:S(2)}) async-start(), calls=%async_computation.9 | async-start | bytes 8192000 | tf_op jit(solution)/shard_map/all_gather | solution.py:585
  45.5 28.7 %collective-permute-start.5 = (bf16[160,3840]{1,0:T(8,128)(2,1)S(1)}, bf16[160,3840]{1,0:T(8,128)(2,1)S(1)}, u32[]{:S(2)}, u32[]{:S(2)}) collective-permute-start(bf16[160,3840]{1,0:T(8,128)(2,1)S(1)} %concatenate.146), channel_id=1, source_target_pairs={{0,16},{8,0},{24,8},{16,24},{1,17},{9,1},{25,9},{17,25},{2,18},{10... | collective-permute-start | bytes 3686408 | tf_op jit(solution)/shard_map/ppermute | solution.py:49
  47.1 28.8 %collective-permute-start.4 = (bf16[160,3840]{1,0:T(8,128)(2,1)S(1)}, bf16[160,3840]{1,0:T(8,128)(2,1)S(1)}, u32[]{:S(2)}, u32[]{:S(2)}) collective-permute-start(bf16[160,3840]{1,0:T(8,128)(2,1)S(1)} %concatenate.146), channel_id=1, source_target_pairs={{0,8},{8,24},{24,16},{16,0},{1,9},{9,25},{25,17},{17,1},{2,10},{10... | collective-permute-start | bytes 3686408 | tf_op jit(solution)/shard_map/ppermute | solution.py:49
  91.6 185.4 %all-gather.11.cloned.1.call-start = ((), (), s32[]{:S(2)}) async-start(), calls=%async_computation.11 | async-start | bytes 8192000 | tf_op jit(solution)/shard_map/all_gather | solution.py:596
  136.1 51.9 %all-to-all-start = ((bf16[4,256,1024]{2,1,0:T(8,128)(2,1)}), bf16[4,256,1024]{2,1,0:T(8,128)(2,1)S(1)}, u32[]{:S(2)}, u32[]{:S(2)}) async-start(bf16[4,256,1024]{2,1,0:T(8,128)(2,1)} %shard_map.594), calls=%async_computation | async-start | bytes 4194304 | tf_op jit(solution)/shard_map/all_to_all | solution.py:429
  139.7 217.0 %reduce-scatter.5.cloned.1.call-start = ((), (), s32[]{:S(2)}) async-start(), calls=%async_computation.12 | async-start | bytes 8192000 | tf_op jit(solution)/shard_map/reduce_scatter | solution.py:616
  257.7 181.5 %reduce-scatter.7.cloned.1.call-start = ((), (), s32[]{:S(2)}) async-start(), calls=%async_computation.13 | async-start | bytes 8192000 | tf_op jit(solution)/shard_map/reduce_scatter | solution.py:628
  326.5 25.5 %all-to-all-start.2 = ((bf16[4,256,384]{2,1,0:T(8,128)(2,1)}), bf16[4,256,384]{2,1,0:T(8,128)(2,1)}, u32[]{:S(2)}, u32[]{:S(2)}) async-start(bf16[4,256,384]{2,1,0:T(8,128)(2,1)} %shard_map.598), calls=%async_computation.2 | async-start | bytes 1572864 | tf_op jit(solution)/shard_map/all_to_all | solution.py:429
  374.9 53.1 %all-to-all-start.3 = ((bf16[4,256,1024]{2,1,0:T(8,128)(2,1)}), bf16[4,256,1024]{2,1,0:T(8,128)(2,1)}, u32[]{:S(2)}, u32[]{:S(2)}) async-start(bf16[4,256,1024]{2,1,0:T(8,128)(2,1)} %shard_map.599), calls=%async_computation.4 | async-start | bytes 4194304 | tf_op jit(solution)/shard_map/all_to_all | solution.py:435
  379.6 157.9 %reduce-scatter.11.cloned.1.call-start = ((), (), s32[]{:S(2)}) async-start(), calls=%async_computation.15 | async-start | bytes 2457600 | tf_op jit(solution)/shard_map/reduce_scatter | solution.py:331
  393.1 19.1 %collective-permute-start.28 = (bf16[160,1280]{1,0:T(8,128)(2,1)}, bf16[160,1280]{1,0:T(8,128)(2,1)}, u32[]{:S(2)}, u32[]{:S(2)}) collective-permute-start(bf16[160,1280]{1,0:T(8,128)(2,1)} %get-tuple-element.89), channel_id=1, source_target_pairs={{0,16},{8,0},{24,8},{16,24},{1,17},{9,1},{25,9},{17,25},{2,18},{10... | collective-permute-start | bytes 1228808 | tf_op jit(solution)/shard_map/ppermute | solution.py:49
  396.7 60.7 %collective-permute-start.26 = (bf16[256,640]{1,0:T(8,128)(2,1)}, bf16[256,640]{1,0:T(8,128)(2,1)}, u32[]{:S(2)}, u32[]{:S(2)}) collective-permute-start(bf16[256,640]{1,0:T(8,128)(2,1)} %get-tuple-element.202), channel_id=1, source_target_pairs={{0,4},{4,0},{1,5},{5,1},{2,6},{6,2},{3,7},{7,3},{8,12},{12,8},{9,1... | collective-permute-start | bytes 983048 | tf_op jit(solution)/shard_map/ppermute | solution.py:53
  399.0 155.0 %reduce-scatter.9.cloned.1.call-start = ((), (), s32[]{:S(2)}) async-start(), calls=%async_computation.14 | async-start | bytes 2048000 | tf_op jit(solution)/shard_map/reduce_scatter | solution.py:331
  439.3 18.2 %collective-permute-start.29 = (bf16[256,3840]{1,0:T(8,128)(2,1)}, bf16[256,3840]{1,0:T(8,128)(2,1)}, u32[]{:S(2)}, u32[]{:S(2)}) collective-permute-start(bf16[256,3840]{1,0:T(8,128)(2,1)} %shard_map.600), channel_id=1, source_target_pairs={{0,4},{4,0},{1,5},{5,1},{2,6},{6,2},{3,7},{7,3},{8,12},{12,8},{9,1... | collective-permute-start | bytes 5898248 | tf_op jit(solution)/shard_map/ppermute | solution.py:53
  455.1 51.7 %collective-permute-start.44 = (bf16[160,320]{1,0:T(8,128)(2,1)}, bf16[160,320]{1,0:T(8,128)(2,1)S(1)}, u32[]{:S(2)}, u32[]{:S(2)}) collective-permute-start(bf16[160,320]{1,0:T(8,128)(2,1)} %get-tuple-element.95), channel_id=1, source_target_pairs={{0,1},{1,2},{2,3},{3,0},{4,5},{5,6},{6,7},{7,4},{8,9},{9,10},{10,1... | collective-permute-start | bytes 307208 | tf_op jit(solution)/shard_map/ppermute | solution.py:58
  491.8 20.9 %collective-permute-start.46 = (bf16[160,320]{1,0:T(8,128)(2,1)S(1)}, bf16[160,320]{1,0:T(8,128)(2,1)S(1)}, u32[]{:S(2)}, u32[]{:S(2)}) collective-permute-start(bf16[160,320]{1,0:T(8,128)(2,1)S(1)} %copy-done.54), channel_id=1, source_target_pairs={{0,3},{1,0},{2,1},{3,2},{4,7},{5,4},{6,5},{7,6},{8,11},{9,8},{10,9... | collective-permute-start | bytes 307208 | tf_op jit(solution)/shard_map/ppermute | solution.py:58
  506.8 30.7 %collective-permute-start.35 = (bf16[80,960]{1,0:T(8,128)(2,1)S(1)}, bf16[80,960]{1,0:T(8,128)(2,1)S(1)}, u32[]{:S(2)}, u32[]{:S(2)}) collective-permute-start(bf16[80,960]{1,0:T(8,128)(2,1)S(1)} %get-tuple-element.208), channel_id=1, source_target_pairs={{0,2},{1,3},{2,0},{3,1},{4,6},{5,7},{6,4},{7,5},{8,10},{9,11},{10,... | collective-permute-start | bytes 460808 | tf_op jit(solution)/shard_map/ppermute | solution.py:58
  506.8 30.7 %collective-permute-start.34 = (bf16[80,960]{1,0:T(8,128)(2,1)S(1)}, bf16[80,960]{1,0:T(8,128)(2,1)S(1)}, u32[]{:S(2)}, u32[]{:S(2)}) collective-permute-start(bf16[80,960]{1,0:T(8,128)(2,1)S(1)} %get-tuple-element.206), channel_id=1, source_target_pairs={{0,1},{1,2},{2,3},{3,0},{4,5},{5,6},{6,7},{7,4},{8,9},{9,10},{10,1... | collective-permute-start | bytes 460808 | tf_op jit(solution)/shard_map/ppermute | solution.py:58
  508.7 46.5 %collective-permute-start.40 = (bf16[80,3840]{1,0:T(8,128)(2,1)}, bf16[80,3840]{1,0:T(8,128)(2,1)}, u32[]{:S(2)}, u32[]{:S(2)}) collective-permute-start(bf16[80,3840]{1,0:T(8,128)(2,1)} %get-tuple-element.94), channel_id=1, source_target_pairs={{0,16},{8,0},{24,8},{16,24},{1,17},{9,1},{25,9},{17,25},{2,18},{10... | collective-permute-start | bytes 1843208 | tf_op jit(solution)/shard_map/ppermute | solution.py:49
  512.7 42.5 %collective-permute-start.39 = (bf16[80,3840]{1,0:T(8,128)(2,1)}, bf16[80,3840]{1,0:T(8,128)(2,1)}, u32[]{:S(2)}, u32[]{:S(2)}) collective-permute-start(bf16[80,3840]{1,0:T(8,128)(2,1)} %get-tuple-element.93), channel_id=1, source_target_pairs={{0,8},{8,24},{24,16},{16,0},{1,9},{9,25},{25,17},{17,1},{2,10},{10... | collective-permute-start | bytes 1843208 | tf_op jit(solution)/shard_map/ppermute | solution.py:49
  (138 other events, 1096.7 us)
Sparse Core Ops, SparseCore 0:
  43.1 38.5 all-gather.4
  83.8 37.1 all-gather.8
  122.9 79.4 all-gather.6
  204.1 72.9 all-gather.10
  279.9 76.7 reduce-scatter.4
  359.6 79.5 reduce-scatter.6
  441.6 47.6 reduce-scatter.10
  491.5 46.4 reduce-scatter.8
